TPU v7x, 256 devices: a whole 4x4x8 slice. The times are simulated.
256 devices in a mesh: expert: 32 (over z, y), loop: 8 (over x, core).
Axes of the slice: x: 4, y: 4, z: 8, core: 2. Of those that a mesh axis runs over, the one named last changes fastest.
Arguments:
- tokens: bfloat16 [4096, 5120], P('expert', 'loop'), may hold values from -6 to 6
- routes: int32 [4096, 6], P('expert'), may hold values from 0 to 31, all different within a row; in each aligned block of 128 rows (0 to 127, 128 to 255, ...) at most 32 rows name the same one
- route_weights: float32 [4096, 6], P('expert'), may hold values from 0.1 to 1
- gate_w: bfloat16 [32, 1536, 5120], P('expert', 'loop'), may hold values from -0.078125 to 0.078125
- up_w: bfloat16 [32, 1536, 5120], P('expert', 'loop'), may hold values from -0.078125 to 0.078125
- down_w: bfloat16 [32, 1536, 5120], P('expert', 'loop'), may hold values from -0.15625 to 0.15625
- shared_gate: bfloat16 [1536, 5120], P('loop'), may hold values from -0.078125 to 0.078125
- shared_up: bfloat16 [1536, 5120], P('loop'), may hold values from -0.078125 to 0.078125
- shared_down: bfloat16 [1536, 5120], P('loop'), may hold values from -0.15625 to 0.15625
Outputs:
- moe_out: bfloat16 [4096, 5120], P('expert', 'loop')
Inputs may be any that keep to these rules, and one draw needn't show every extreme that they name: `routes`: within the rows of one device (aligned blocks of 128 rows) no expert is named by more than 32 rows; the 6 experts of a row differ.
All inputs are finite; a program needn't handle non-finite values.
Results may differ from a plain program's by a relative error of at most 0.02.
Values may be sent and summed in bfloat16 or wider, within the bound.
No kernel may reach another device: no remote copies, remote signals or barrier semaphores. Data moves between devices by JAX's collectives and lax.ppermute only.
A program may use at most 128 MiB of HBM per device.

v0:
```python
import jax
import jax.numpy as jnp
from jax import lax
from jax.sharding import PartitionSpec as P


def project_rows(rows, weight):
    return lax.dot_general(
        rows, weight, (((1,), (1,)), ((), ())), preferred_element_type=jnp.float32
    )


def local(tokens, routes, route_weights, gate_w, up_w, down_w, shared_gate, shared_up, shared_down):
    tok_rows = tokens.shape[0]
    top_count = routes.shape[1]
    groups = lax.axis_size("expert")
    capacity = tok_rows * top_count * 4 // (3 * groups)
    slot_total = groups * capacity
    gathered = lax.all_gather(tokens, "loop", axis=1, tiled=True)
    flat_routes = routes.reshape(-1)
    onehot = (flat_routes[:, None] == jnp.arange(groups, dtype=jnp.int32)[None, :]).astype(
        jnp.int32
    )
    before = jnp.cumsum(onehot, axis=0) - onehot
    position = jnp.sum(before * onehot, axis=1)
    slot_index = (flat_routes * capacity + position).reshape(tok_rows, top_count)
    slot_ids = jnp.arange(slot_total, dtype=jnp.int32)
    matches = slot_ids[:, None, None] == slot_index[None, :, :]
    selector = jnp.sum(matches.astype(jnp.float32), axis=2).astype(jnp.bfloat16)
    combine_w = jnp.sum(jnp.where(matches, route_weights[None, :, :], 0.0), axis=2)
    combine_high = combine_w.astype(jnp.bfloat16)
    combine_low = (combine_w - combine_high.astype(jnp.float32)).astype(jnp.bfloat16)
    shared_gate_act = project_rows(gathered, shared_gate)
    shared_up_act = project_rows(gathered, shared_up)
    shared_hidden = (jax.nn.silu(shared_gate_act) * shared_up_act).astype(jnp.bfloat16)
    w_gate = gate_w[0]
    w_up = up_w[0]
    w_down = down_w[0]
    outgoing = jnp.dot(selector, gathered, preferred_element_type=jnp.float32).astype(jnp.bfloat16)
    incoming = lax.all_to_all(outgoing, "expert", split_axis=0, concat_axis=0, tiled=True)
    gate_act = project_rows(incoming, w_gate)
    up_act = project_rows(incoming, w_up)
    hidden = (jax.nn.silu(gate_act) * up_act).astype(jnp.bfloat16)
    routed_term = jnp.einsum("fc,rf->cr", w_down, hidden, preferred_element_type=jnp.float32)
    shared_term = jnp.einsum(
        "fc,rf->cr", shared_down, shared_hidden, preferred_element_type=jnp.float32
    )
    summed = lax.psum_scatter(
        jnp.concatenate([routed_term, shared_term], axis=1).astype(jnp.bfloat16),
        "loop",
        scatter_dimension=0,
        tiled=True,
    ).astype(jnp.float32)
    expert_result = summed[:, :slot_total].astype(jnp.bfloat16)
    shared_part = summed[:, slot_total:]
    returned = lax.all_to_all(expert_result, "expert", split_axis=1, concat_axis=1, tiled=True)
    routed_part = jnp.dot(returned, combine_high, preferred_element_type=jnp.float32) + jnp.dot(
        returned, combine_low, preferred_element_type=jnp.float32
    )
    return (routed_part + shared_part).T.astype(jnp.bfloat16)


def solution(mesh):
    placed = (
        P("expert", "loop"),
        P("expert", None),
        P("expert", None),
        P("expert", "loop", None),
        P("expert", "loop", None),
        P("expert", "loop", None),
        P("loop", None),
        P("loop", None),
        P("loop", None),
    )
    return jax.shard_map(
        local, mesh=mesh, in_specs=placed, out_specs=P("expert", "loop"), check_vma=False
    )
```

profile of v0, /device:TPU:3, one launch (start us, length us, event | category | flops | bytes accessed | tf_op | source)
XLA Modules:
  0.0 481.5 jit_solution(17969575525954098838)
XLA Ops:
  6.5 0.7 all-gather.2.cloned.1.call-update
  7.3 0.8 copy.38
  8.3 1.7 reduce-window.6
  10.1 0.3 slice_reduce_fusion
  10.7 0.7 multiply_add_fusion
  11.4 2.2 select_reduce_fusion
  13.6 23.9 %all-gather.2.cloned.1.call-done = bf16[128,5120]{1,0:T(8,128)(2,1)} async-done(((bf16[128,640]{1,0:T(8,128)(2,1)}), bf16[128,5120]{1,0:T(8,128)(2,1)}) %all-gather.2.cloned.1.call-update) | async-done | bytes 1310736 | tf_op jit(solution)/shard_map/all_gather | solution.py:19
  37.5 6.7 %convolution_convert_fusion = bf16[1024,5120]{1,0:T(8,128)(2,1)} fusion(bf16[128,5120]{1,0:T(8,128)(2,1)} %all-gather.2.cloned.1.call-done, bf16[1024,128]{1,0:T(8,128)(2,1)S(1)} %get-tuple-element.6), kind=kOutput, calls=%fused_computation.2 | convolution fusion | flops 1347420160 | bytes 12058624 | tf_op jit(solution)/shard_map/dot_general | solution.py:39
  44.2 9.8 %all-to-all-start = ((bf16[32,32,5120]{2,1,0:T(8,128)(2,1)}), bf16[32,32,5120]{2,1,0:T(8,128)(2,1)}, u32[]{:S(2)}, u32[]{:S(2)}) async-start(bf16[32,32,5120]{2,1,0:T(8,128)(2,1)} %bitcast.57), calls=%async_computation | async-start | bytes 20971520 | tf_op jit(solution)/shard_map/all_to_all | solution.py:40
  54.0 0.2 reduce-scatter.4.cloned.1.call-start
  54.3 2.2 fusion.40
  56.5 5.1 %fusion = bf16[5120,128]{0,1:T(8,128)(2,1)} fusion(bf16[192,5120]{1,0:T(8,128)(2,1)} %param.17, bf16[128,5120]{1,0:T(8,128)(2,1)S(1)} %copy-done.2, bf16[192,5120]{1,0:T(8,128)(2,1)} %param.16, f32[128,192]{0,1:T(8,128)S(1)} %fusion.40), kind=kOutput, calls=%fused_computation.4 | convolution fusion | flops 504119296 | bytes 6651904 | tf_op jit(solution)/shard_map/fc,rf->cr/dot_general | solution.py:45
  61.6 227.4 %all-to-all-done = bf16[32,32,5120]{2,1,0:T(8,128)(2,1)} async-done(((bf16[32,32,5120]{2,1,0:T(8,128)(2,1)}), bf16[32,32,5120]{2,1,0:T(8,128)(2,1)}, u32[]{:S(2)}, u32[]{:S(2)}) %all-to-all-start) | async-done | bytes 10485792 | tf_op jit(solution)/shard_map/all_to_all | solution.py:40
  289.0 9.0 %fusion.4 = f32[1024,192]{0,1:T(8,128)} fusion(bf16[1024,5120]{1,0:T(8,128)(2,1)} %bitcast.2, bf16[1,192,5120]{2,1,0:T(8,128)(2,1)} %param.12), kind=kOutput, calls=%fused_computation.11 | convolution fusion | flops 2013265920 | bytes 13238272 | tf_op jit(solution)/shard_map/dot_general | solution.py:8
  298.0 17.3 %convert_bitcast_fusion = bf16[5120,1024]{0,1:T(8,128)(2,1)} fusion(bf16[1,192,5120]{2,1,0:T(8,128)(2,1)S(1)} %copy-done, bf16[1024,5120]{1,0:T(8,128)(2,1)} %bitcast.2, bf16[1,192,5120]{2,1,0:T(8,128)(2,1)} %param.13, f32[1024,192]{0,1:T(8,128)} %fusion.4), kind=kOutput, calls=%fused_computation.1 | convolution fusion | flops 4032954368 | bytes 25690112 | tf_op jit(solution)/shard_map/fc,rf->cr/dot_general | solution.py:44
  315.3 12.7 %pad_maximum_fusion = bf16[5120,1152]{0,1:T(8,128)(2,1)} fusion(bf16[5120,128]{0,1:T(8,128)(2,1)S(1)} %copy-done.3, bf16[5120,1024]{0,1:T(8,128)(2,1)} %convert_bitcast_fusion), kind=kLoop, calls=%fused_computation | loop fusion | flops 23592960 | bytes 23592960 | tf_op jit(solution)/shard_map/concatenate | solution.py:49
  328.1 15.3 %copy.44 = bf16[5120,1152]{1,0:T(8,128)(2,1)} copy(bf16[5120,1152]{0,1:T(8,128)(2,1)} %pad_maximum_fusion) | data formatting | bytes 23592960
  343.4 82.0 %reduce-scatter.4.cloned.1.call-done = bf16[640,1152]{1,0:T(8,128)(2,1)} async-done(((bf16[5120,1152]{1,0:T(8,128)(2,1)}), bf16[640,1152]{1,0:T(8,128)(2,1)}) %reduce-scatter.4.cloned.1.call-update) | async-done | bytes 1474576 | tf_op jit(solution)/shard_map/reduce_scatter | solution.py:48
  425.4 1.3 slice-done
  426.7 0.7 copy.46
  427.5 45.3 %all_to_all.24 = bf16[640,32,32]{0,2,1:T(8,128)(2,1)S(1)} all-to-all(bf16[640,32,32]{0,2,1:T(8,128)(2,1)S(1)} %bitcast.60), channel_id=1, replica_groups=mesh['expert'=32,'loop'=8] {'expert'}, dimensions={1} | all-to-all | bytes 2621440 | tf_op jit(solution)/shard_map/all_to_all | solution.py:56
  472.7 0.5 fusion.26
  473.3 0.5 fusion.16
  473.8 0.8 copy.43
  (22 shorter events, 0.6 us)
Async XLA Ops:
  6.5 291.4 %copy-start = (bf16[1,192,5120]{2,1,0:T(8,128)(2,1)S(1)}, bf16[1,192,5120]{2,1,0:T(8,128)(2,1)}, u32[]{:S(2)}) copy-start(bf16[1,192,5120]{2,1,0:T(8,128)(2,1)} %param.14) | copy-start | bytes 5898244
  6.5 31.0 %all-gather.2.cloned.1.call-start = ((), (), s32[]{:S(2)}) async-start(), calls=%async_computation.3 | async-start | bytes 1474560 | tf_op jit(solution)/shard_map/all_gather | solution.py:19
  44.2 10.1 %copy-start.2 = (bf16[128,5120]{1,0:T(8,128)(2,1)S(1)}, bf16[128,5120]{1,0:T(8,128)(2,1)}, u32[]{:S(2)}) copy-start(bf16[128,5120]{1,0:T(8,128)(2,1)} %all-gather.2.cloned.1.call-done) | copy-start | bytes 3932164
  44.2 244.8 %all-to-all-start = ((bf16[32,32,5120]{2,1,0:T(8,128)(2,1)}), bf16[32,32,5120]{2,1,0:T(8,128)(2,1)}, u32[]{:S(2)}, u32[]{:S(2)}) async-start(bf16[32,32,5120]{2,1,0:T(8,128)(2,1)} %bitcast.57), calls=%async_computation | async-start | bytes 20971520 | tf_op jit(solution)/shard_map/all_to_all | solution.py:40
  54.0 371.4 %reduce-scatter.4.cloned.1.call-start = ((), (), s32[]{:S(2)}) async-start(), calls=%async_computation.4 | async-start | bytes 13271040 | tf_op jit(solution)/shard_map/reduce_scatter | solution.py:48
  298.0 17.3 %copy-start.3 = (bf16[5120,128]{0,1:T(8,128)(2,1)S(1)}, bf16[5120,128]{0,1:T(8,128)(2,1)}, u32[]{:S(2)}) copy-start(bf16[5120,128]{0,1:T(8,128)(2,1)} %fusion) | copy-start | bytes 3932164
  425.4 1.3 slice-start
  427.4 45.3 %copy-start.5 = (f32[1024,128]{1,0:T(8,128)S(1)}, f32[1024,128]{1,0:T(8,128)}, u32[]{:S(2)}) copy-start(f32[1024,128]{1,0:T(8,128)} %get-tuple-element.5) | copy-start | bytes 1572868
  427.4 45.8 %copy-start.4 = (bf16[640,1152]{1,0:T(8,128)(2,1)S(1)}, bf16[640,1152]{1,0:T(8,128)(2,1)}, u32[]{:S(2)}) copy-start(bf16[640,1152]{1,0:T(8,128)(2,1)} %reduce-scatter.4.cloned.1.call-done) | copy-start | bytes 4423684
  472.7 1.9 copy-start.1
Sparse Core Ops, SparseCore 0:
  9.2 28.2 all-gather.1
  343.5 81.8 reduce-scatter.3
where the time goes:
time: 482 us; the launch traced here: 481 us
  waiting for transfers between devices  334 us (69%)
  blocking collectives  45.3 us (9%)
  matrix products  41.4 us (9%)
  local copies, waits for them, and re-layouts  19.6 us (4%)
  other arithmetic  17.5 us (4%)
  between operations  13.5 us (3%)
  starting transfers between devices  10 us (2%)
    all_to_all x1, waiting for transfers between devices, local(): lax.all_to_all(outgoing, 'expert', split_axis=0, concat_axis=0, tiled=True)  227 us
    reduce_scatter x1, waiting for transfers between devices, local(): lax.psum_scatter(jnp.concatenate([routed_term, shared_term], axis=1).asty...  82 us
    all_to_all x1, blocking collectives, local(): lax.all_to_all(expert_result, 'expert', split_axis=1, concat_axis=1, tile...  45.3 us
    all_gather x1, waiting for transfers between devices, local(): gathered = lax.all_gather(tokens, 'loop', axis=1, tiled=True)  23.9 us
    dot_general x1, matrix products, local(): jnp.einsum('fc,rf->cr', w_down, hidden, preferred_element_type=jnp.float32)  17.3 us
    unnamed x15, local copies, waits for them, and re-layouts  16.8 us
    concatenate x1, other arithmetic, local(): jnp.concatenate([routed_term, shared_term], axis=1).astype(jnp.bfloat16)  12.7 us
    dot_general x2, matrix products, project_rows(): lax.dot_general(rows, weight, (((1,), (1,)), ((), ())), preferred_element...  11.2 us
  transfers between devices with their start and end apart: 3, of which 3 were waited for; matrix products, arithmetic and copies ran while one was open for 3% of the time, Pallas kernels for 0%

commit v1 on v0

--- a/solution.py
+++ b/solution.py
@@ -53,7 +53,12 @@
     ).astype(jnp.float32)
     expert_result = summed[:, :slot_total].astype(jnp.bfloat16)
     shared_part = summed[:, slot_total:]
-    returned = lax.all_to_all(expert_result, "expert", split_axis=1, concat_axis=1, tiled=True)
+    returned = jnp.concatenate(
+        lax.all_to_all(
+            jnp.stack(jnp.split(expert_result, lax.axis_size("expert"), axis=1)), "expert", 0, 0
+        ),
+        axis=1,
+    )
     routed_part = jnp.dot(returned, combine_high, preferred_element_type=jnp.float32) + jnp.dot(
         returned, combine_low, preferred_element_type=jnp.float32
     )

time: 482 us -> 535 us (1.11)
  local copies, waits for them, and re-layouts: 19.6 us -> 69.9 us
    unnamed x15 -> x107, local copies, waits for them, and re-layouts: 16.8 us -> 63 us
where the time goes in v1:
time: 535 us; the launch traced here: 533 us
  waiting for transfers between devices  334 us (62%)
  local copies, waits for them, and re-layouts  69.9 us (13%)
  blocking collectives  45.2 us (8%)
  matrix products  42.2 us (8%)
  other arithmetic  17.5 us (3%)
  between operations  13.7 us (3%)
  starting transfers between devices  9.86 us (2%)
    all_to_all x1, waiting for transfers between devices, local(): lax.all_to_all(outgoing, 'expert', split_axis=0, concat_axis=0, tiled=True)  228 us
    reduce_scatter x1, waiting for transfers between devices, local(): lax.psum_scatter(jnp.concatenate([routed_term, shared_term], axis=1).asty...  82 us
    unnamed x107, local copies, waits for them, and re-layouts  63 us
    all_to_all x1, blocking collectives, local(): lax.all_to_all(jnp.stack(jnp.split(expert_result, lax.axis_size('expert')...  45.2 us
    all_gather x1, waiting for transfers between devices, local(): gathered = lax.all_gather(tokens, 'loop', axis=1, tiled=True)  24 us
    dot_general x1, matrix products, local(): jnp.einsum('fc,rf->cr', w_down, hidden, preferred_element_type=jnp.float32)  17.5 us
    concatenate x1, other arithmetic, local(): jnp.concatenate([routed_term, shared_term], axis=1).astype(jnp.bfloat16)  12.7 us
    dot_general x2, matrix products, project_rows(): lax.dot_general(rows, weight, (((1,), (1,)), ((), ())), preferred_element...  11.2 us
  transfers between devices with their start and end apart: 3, of which 3 were waited for; matrix products, arithmetic and copies ran while one was open for 3% of the time, Pallas kernels for 0%

profile of v1, /device:TPU:3, one launch (start us, length us, event | category | flops | bytes accessed | tf_op | source)
XLA Modules:
  0.0 532.7 jit_solution(4161392724276874686)
XLA Ops:
  8.3 1.7 reduce-window.6
  11.4 2.2 select_reduce_fusion
  13.6 24.0 %all-gather.2.cloned.1.call-done = bf16[128,5120]{1,0:T(8,128)(2,1)} async-done(((bf16[128,640]{1,0:T(8,128)(2,1)}), bf16[128,5120]{1,0:T(8,128)(2,1)}) %all-gather.2.cloned.1.call-update) | async-done | bytes 1310736 | tf_op jit(solution)/shard_map/all_gather | solution.py:19
  37.5 6.7 %convolution_convert_fusion = bf16[1024,5120]{1,0:T(8,128)(2,1)} fusion(bf16[128,5120]{1,0:T(8,128)(2,1)} %all-gather.2.cloned.1.call-done, bf16[1024,128]{1,0:T(8,128)(2,1)S(1)} %get-tuple-element.6), kind=kOutput, calls=%fused_computation.2 | convolution fusion | flops 1347420160 | bytes 12058624 | tf_op jit(solution)/shard_map/dot_general | solution.py:39
  44.2 9.8 %all-to-all-start = ((bf16[32,32,5120]{2,1,0:T(8,128)(2,1)}), bf16[32,32,5120]{2,1,0:T(8,128)(2,1)}, u32[]{:S(2)}, u32[]{:S(2)}) async-start(bf16[32,32,5120]{2,1,0:T(8,128)(2,1)} %bitcast.122), calls=%async_computation | async-start | bytes 20971520 | tf_op jit(solution)/shard_map/all_to_all | solution.py:40
  54.1 2.2 fusion.42
  56.3 5.1 fusion
  61.4 227.6 %all-to-all-done = bf16[32,32,5120]{2,1,0:T(8,128)(2,1)} async-done(((bf16[32,32,5120]{2,1,0:T(8,128)(2,1)}), bf16[32,32,5120]{2,1,0:T(8,128)(2,1)}, u32[]{:S(2)}, u32[]{:S(2)}) %all-to-all-start) | async-done | bytes 10485792 | tf_op jit(solution)/shard_map/all_to_all | solution.py:40
  289.0 9.0 %fusion.4 = f32[1024,192]{0,1:T(8,128)} fusion(bf16[1024,5120]{1,0:T(8,128)(2,1)} %bitcast.2, bf16[1,192,5120]{2,1,0:T(8,128)(2,1)} %param.12), kind=kOutput, calls=%fused_computation.11 | convolution fusion | flops 2013265920 | bytes 13238272 | tf_op jit(solution)/shard_map/dot_general | solution.py:8
  298.0 17.5 %convert_bitcast_fusion = bf16[5120,1024]{0,1:T(8,128)(2,1)} fusion(bf16[1,192,5120]{2,1,0:T(8,128)(2,1)S(1)} %copy-done, bf16[1024,5120]{1,0:T(8,128)(2,1)} %bitcast.2, bf16[1,192,5120]{2,1,0:T(8,128)(2,1)} %param.13, f32[1024,192]{0,1:T(8,128)} %fusion.4), kind=kOutput, calls=%fused_computation.1 | convolution fusion | flops 4032954368 | bytes 25690112 | tf_op jit(solution)/shard_map/fc,rf->cr/dot_general | solution.py:44
  315.5 12.7 %pad_maximum_fusion = bf16[5120,1152]{0,1:T(8,128)(2,1)} fusion(bf16[5120,128]{0,1:T(8,128)(2,1)S(1)} %copy-done.4, bf16[5120,1024]{0,1:T(8,128)(2,1)} %convert_bitcast_fusion), kind=kLoop, calls=%fused_computation | loop fusion | flops 23592960 | bytes 23592960 | tf_op jit(solution)/shard_map/concatenate | solution.py:49
  328.2 15.7 %copy.44 = bf16[5120,1152]{1,0:T(8,128)(2,1)} copy(bf16[5120,1152]{0,1:T(8,128)(2,1)} %pad_maximum_fusion) | data formatting | bytes 23592960
  343.9 82.0 %reduce-scatter.4.cloned.1.call-done = bf16[640,1152]{1,0:T(8,128)(2,1)} async-done(((bf16[5120,1152]{1,0:T(8,128)(2,1)}), bf16[640,1152]{1,0:T(8,128)(2,1)}) %reduce-scatter.4.cloned.1.call-update) | async-done | bytes 1474576 | tf_op jit(solution)/shard_map/reduce_scatter | solution.py:48
  425.9 2.3 fusion.41
  437.2 2.1 fusion.40
  441.4 1.6 copy.75
  444.7 1.6 copy.73
  446.3 1.6 copy.72
  451.2 1.6 copy.69
  456.1 1.6 copy.66
  457.8 1.6 copy.65
  461.1 1.7 copy.63
  477.2 45.2 %all_to_all.17 = bf16[32,640,32]{1,2,0:T(8,128)(2,1)S(1)} all-to-all(bf16[32,640,32]{1,2,0:T(8,128)(2,1)S(1)} %constant_dynamic-update-slice_fusion), channel_id=1, replica_groups=mesh['expert'=32,'loop'=8] {'expert'}, dimensions={0} | all-to-all | bytes 2621440 | tf_op jit(solution)/shard_map/all_to_all | solution.py:57
  524.2 1.7 copy.43
  (115 shorter events, 39.9 us)
Async XLA Ops:
  6.5 291.5 %copy-start = (bf16[1,192,5120]{2,1,0:T(8,128)(2,1)S(1)}, bf16[1,192,5120]{2,1,0:T(8,128)(2,1)}, u32[]{:S(2)}) copy-start(bf16[1,192,5120]{2,1,0:T(8,128)(2,1)} %param.14) | copy-start | bytes 5898244
  6.5 31.0 %all-gather.2.cloned.1.call-start = ((), (), s32[]{:S(2)}) async-start(), calls=%async_computation.3 | async-start | bytes 1474560 | tf_op jit(solution)/shard_map/all_gather | solution.py:19
  44.2 9.9 %copy-start.3 = (bf16[128,5120]{1,0:T(8,128)(2,1)S(1)}, bf16[128,5120]{1,0:T(8,128)(2,1)}, u32[]{:S(2)}) copy-start(bf16[128,5120]{1,0:T(8,128)(2,1)} %all-gather.2.cloned.1.call-done) | copy-start | bytes 3932164
  44.2 244.8 %all-to-all-start = ((bf16[32,32,5120]{2,1,0:T(8,128)(2,1)}), bf16[32,32,5120]{2,1,0:T(8,128)(2,1)}, u32[]{:S(2)}, u32[]{:S(2)}) async-start(bf16[32,32,5120]{2,1,0:T(8,128)(2,1)} %bitcast.122), calls=%async_computation | async-start | bytes 20971520 | tf_op jit(solution)/shard_map/all_to_all | solution.py:40
  54.0 371.9 %reduce-scatter.4.cloned.1.call-start = ((), (), s32[]{:S(2)}) async-start(), calls=%async_computation.4 | async-start | bytes 13271040 | tf_op jit(solution)/shard_map/reduce_scatter | solution.py:48
  298.0 17.5 %copy-start.4 = (bf16[5120,128]{0,1:T(8,128)(2,1)S(1)}, bf16[5120,128]{0,1:T(8,128)(2,1)}, u32[]{:S(2)}) copy-start(bf16[5120,128]{0,1:T(8,128)(2,1)} %fusion) | copy-start | bytes 3932164
  429.0 8.2 %copy-start.2 = (bf16[640,1152]{1,0:T(8,128)(2,1)S(1)}, bf16[640,1152]{1,0:T(8,128)(2,1)}, u32[]{:S(2)}) copy-start(bf16[640,1152]{1,0:T(8,128)(2,1)} %reduce-scatter.4.cloned.1.call-done) | copy-start | bytes 4423684
  463.5 10.2 %copy-start.8 = (bf16[640,32]{0,1:T(8,128)(2,1)S(1)}, bf16[640,32]{0,1:T(8,128)(2,1)}, u32[]{:S(2)}) copy-start(bf16[640,32]{0,1:T(8,128)(2,1)} %copy.57) | copy-start | bytes 122884
  463.5 10.2 %copy-start.6 = (bf16[640,32]{0,1:T(8,128)(2,1)S(1)}, bf16[640,32]{0,1:T(8,128)(2,1)}, u32[]{:S(2)}) copy-start(bf16[640,32]{0,1:T(8,128)(2,1)} %copy.58) | copy-start | bytes 122884
  464.2 12.8 %copy-start.13 = (bf16[640,32]{0,1:T(8,128)(2,1)S(1)}, bf16[640,32]{0,1:T(8,128)(2,1)}, u32[]{:S(2)}) copy-start(bf16[640,32]{0,1:T(8,128)(2,1)} %copy.70) | copy-start | bytes 122884
  464.2 12.8 %copy-start.12 = (bf16[640,32]{0,1:T(8,128)(2,1)S(1)}, bf16[640,32]{0,1:T(8,128)(2,1)}, u32[]{:S(2)}) copy-start(bf16[640,32]{0,1:T(8,128)(2,1)} %copy.71) | copy-start | bytes 122884
  464.2 12.9 %copy-start.11 = (bf16[640,32]{0,1:T(8,128)(2,1)S(1)}, bf16[640,32]{0,1:T(8,128)(2,1)}, u32[]{:S(2)}) copy-start(bf16[640,32]{0,1:T(8,128)(2,1)} %copy.72) | copy-start | bytes 122884
  464.2 12.9 %copy-start.10 = (bf16[640,32]{0,1:T(8,128)(2,1)S(1)}, bf16[640,32]{0,1:T(8,128)(2,1)}, u32[]{:S(2)}) copy-start(bf16[640,32]{0,1:T(8,128)(2,1)} %copy.73) | copy-start | bytes 122884
  464.2 12.9 %copy-start.9 = (bf16[640,32]{0,1:T(8,128)(2,1)S(1)}, bf16[640,32]{0,1:T(8,128)(2,1)}, u32[]{:S(2)}) copy-start(bf16[640,32]{0,1:T(8,128)(2,1)} %copy.74) | copy-start | bytes 122884
  464.2 12.9 %copy-start.7 = (bf16[640,32]{0,1:T(8,128)(2,1)S(1)}, bf16[640,32]{0,1:T(8,128)(2,1)}, u32[]{:S(2)}) copy-start(bf16[640,32]{0,1:T(8,128)(2,1)} %copy.75) | copy-start | bytes 122884
  465.0 11.9 %copy-start.17 = (bf16[640,32]{0,1:T(8,128)(2,1)S(1)}, bf16[640,32]{0,1:T(8,128)(2,1)}, u32[]{:S(2)}) copy-start(bf16[640,32]{0,1:T(8,128)(2,1)} %copy.66) | copy-start | bytes 122884
  465.0 11.9 %copy-start.16 = (bf16[640,32]{0,1:T(8,128)(2,1)S(1)}, bf16[640,32]{0,1:T(8,128)(2,1)}, u32[]{:S(2)}) copy-start(bf16[640,32]{0,1:T(8,128)(2,1)} %copy.67) | copy-start | bytes 122884
  465.0 12.0 %copy-start.15 = (bf16[640,32]{0,1:T(8,128)(2,1)S(1)}, bf16[640,32]{0,1:T(8,128)(2,1)}, u32[]{:S(2)}) copy-start(bf16[640,32]{0,1:T(8,128)(2,1)} %copy.68) | copy-start | bytes 122884
  465.0 12.0 %copy-start.14 = (bf16[640,32]{0,1:T(8,128)(2,1)S(1)}, bf16[640,32]{0,1:T(8,128)(2,1)}, u32[]{:S(2)}) copy-start(bf16[640,32]{0,1:T(8,128)(2,1)} %copy.69) | copy-start | bytes 122884
  465.7 11.1 %copy-start.20 = (bf16[640,32]{0,1:T(8,128)(2,1)S(1)}, bf16[640,32]{0,1:T(8,128)(2,1)}, u32[]{:S(2)}) copy-start(bf16[640,32]{0,1:T(8,128)(2,1)} %copy.63) | copy-start | bytes 122884
  465.7 11.1 %copy-start.19 = (bf16[640,32]{0,1:T(8,128)(2,1)S(1)}, bf16[640,32]{0,1:T(8,128)(2,1)}, u32[]{:S(2)}) copy-start(bf16[640,32]{0,1:T(8,128)(2,1)} %copy.64) | copy-start | bytes 122884
  465.7 11.1 %copy-start.18 = (bf16[640,32]{0,1:T(8,128)(2,1)S(1)}, bf16[640,32]{0,1:T(8,128)(2,1)}, u32[]{:S(2)}) copy-start(bf16[640,32]{0,1:T(8,128)(2,1)} %copy.65) | copy-start | bytes 122884
  477.2 45.2 %copy-start.5 = (f32[1024,128]{1,0:T(8,128)S(1)}, f32[1024,128]{1,0:T(8,128)}, u32[]{:S(2)}) copy-start(f32[1024,128]{1,0:T(8,128)} %get-tuple-element.5) | copy-start | bytes 1572868
  522.4 3.5 copy-start.1
Sparse Core Ops, SparseCore 0:
  9.2 28.2 all-gather.1
  344.0 81.8 reduce-scatter.3
